TPU v7x, 128 devices: a whole 4x4x4 slice. The times are simulated.
128 devices in a mesh: depth: 2 (over x_hi), row: 8 (over z, core), col: 8 (over x_lo, y).
Axes of the slice: x: 4 (x_hi: 2, x_lo: 2; x = x_hi * 2 + x_lo), y: 4, z: 4, core: 2. Of those that a mesh axis runs over, the one named last changes fastest.
Arguments:
- inputs: bfloat16 [1536, 8192], P(('depth', 'col'), 'row'), may hold values from -6 to 6
- grad_out: bfloat16 [1536, 8192], P(('depth', 'col'), 'row'), may hold values from -3 to 3
- gate_weight: bfloat16 [8192, 14336], P('row', 'col'), may hold values from -0.0625 to 0.0625
- up_weight: bfloat16 [8192, 14336], P('row', 'col'), may hold values from -0.0625 to 0.0625
- down_weight: bfloat16 [14336, 8192], P('col', 'row'), may hold values from -0.046875 to 0.046875
Outputs:
- grad_in: bfloat16 [1536, 8192], P(('depth', 'col'), 'row')
- grad_gate: bfloat16 [8192, 14336], P('row', 'col')
- grad_up: bfloat16 [8192, 14336], P('row', 'col')
- grad_down: bfloat16 [14336, 8192], P('col', 'row')
All inputs are finite; a program needn't handle non-finite values.
Results may differ from a plain program's by a relative error of at most 0.03.
Values may be sent and summed in bfloat16 or wider, within the bound.
A program may use at most 128 MiB of HBM per device.

v0:
```python
import jax
import jax.numpy as jnp
from jax import lax
from jax.sharding import PartitionSpec as P


def swiglu_grads(gate_sum, up_sum, hidden_grad):
    sigmoid_gate = jax.nn.sigmoid(gate_sum)
    hidden = (gate_sum * sigmoid_gate * up_sum).astype(jnp.bfloat16)
    grad_gate_act = (
        hidden_grad * up_sum * sigmoid_gate * (1.0 + gate_sum * (1.0 - sigmoid_gate))
    ).astype(jnp.bfloat16)
    grad_up_act = (hidden_grad * gate_sum * sigmoid_gate).astype(jnp.bfloat16)
    return (grad_gate_act, grad_up_act, hidden)


def per_device(inputs, grad_out, gate_weight, up_weight, down_weight):
    contract_last = (((1,), (1,)), ((), ()))
    over_tokens = (((0,), (0,)), ((), ()))
    half_width = gate_weight.shape[1] // lax.axis_size("depth")
    offset = lax.axis_index("depth") * half_width
    gate_cols = lax.dynamic_slice_in_dim(gate_weight, offset, half_width, 1)
    up_cols = lax.dynamic_slice_in_dim(up_weight, offset, half_width, 1)
    down_rows = lax.dynamic_slice_in_dim(down_weight, offset, half_width, 0)
    whole_inputs, whole_grads = (
        lax.all_gather(inputs, ("depth", "col"), axis=0, tiled=True),
        lax.all_gather(grad_out, ("depth", "col"), axis=0, tiled=True),
    )
    gate_part = jnp.dot(whole_inputs, gate_cols, preferred_element_type=jnp.float32)
    up_part = jnp.dot(whole_inputs, up_cols, preferred_element_type=jnp.float32)
    hidden_part = lax.dot_general(
        whole_grads, down_rows, contract_last, preferred_element_type=jnp.float32
    )
    gate_sum, up_sum, hidden_grad = (
        lax.psum(gate_part.astype(jnp.bfloat16), "row").astype(jnp.float32),
        lax.psum(up_part.astype(jnp.bfloat16), "row").astype(jnp.float32),
        lax.psum(hidden_part.astype(jnp.bfloat16), "row").astype(jnp.float32),
    )
    grad_gate_act, grad_up_act, hidden = swiglu_grads(gate_sum, up_sum, hidden_grad)
    gate_grad_full = lax.dot_general(
        whole_inputs, grad_gate_act, over_tokens, preferred_element_type=jnp.float32
    )
    up_grad_full = lax.dot_general(
        whole_inputs, grad_up_act, over_tokens, preferred_element_type=jnp.float32
    )
    down_grad_full = lax.dot_general(
        hidden, whole_grads, over_tokens, preferred_element_type=jnp.float32
    )
    grad_in = lax.psum_scatter(
        (
            lax.dot_general(
                grad_gate_act, gate_cols, contract_last, preferred_element_type=jnp.float32
            )
            + lax.dot_general(
                grad_up_act, up_cols, contract_last, preferred_element_type=jnp.float32
            )
        ).astype(jnp.bfloat16),
        ("depth", "col"),
        scatter_dimension=0,
        tiled=True,
    )
    gate_half, up_half, down_half = (gate_grad_full, up_grad_full, down_grad_full)
    grad_gate, grad_up, grad_down = (
        lax.all_gather(gate_half.astype(jnp.bfloat16), "depth", axis=1, tiled=True),
        lax.all_gather(up_half.astype(jnp.bfloat16), "depth", axis=1, tiled=True),
        lax.all_gather(down_half.astype(jnp.bfloat16), "depth", axis=0, tiled=True),
    )
    return (grad_in, grad_gate, grad_up, grad_down)


def solution(mesh):
    in_specs = (
        P(("depth", "col"), "row"),
        P(("depth", "col"), "row"),
        P("row", "col"),
        P("row", "col"),
        P("col", "row"),
    )
    out_specs = (P(("depth", "col"), "row"), P("row", "col"), P("row", "col"), P("col", "row"))
    return jax.shard_map(
        per_device, mesh=mesh, in_specs=in_specs, out_specs=out_specs, check_vma=False
    )
```

profile of v0, /device:TPU:73, one launch (start us, length us, event | category | flops | bytes accessed | tf_op | source)
XLA Modules:
  0.0 482.3 jit_solution(14102498934541668568)
XLA Ops:
  7.2 0.0 all-gather.8.cloned.1.call-start
  7.2 0.7 all-gather.8.cloned.1.call-update
  7.9 0.0 all-gather.6.cloned.1.call-start
  7.9 0.7 all-gather.6.cloned.1.call-update
  8.6 0.0 all-reduce.3.cloned.1.call-start
  8.7 49.2 %all-gather.8.cloned.1.call-done = bf16[1536,1024]{1,0:T(8,128)(2,1)} async-done(((bf16[96,1024]{1,0:T(8,128)(2,1)}), bf16[1536,1024]{1,0:T(8,128)(2,1)}) %all-gather.8.cloned.1.call-update) | async-done | bytes 3145744 | tf_op jit(solution)/shard_map/all_gather | solution.py:26
  57.9 7.2 %fusion.12 = bf16[1536,896]{0,1:T(8,128)(2,1)} fusion(bf16[1536,1024]{1,0:T(8,128)(2,1)} %all-gather.8.cloned.1.call-done, bf16[1024,1792]{1,0:T(8,128)(2,1)} %param.7, s32[]{:T(128)S(6)} %select_n.2), kind=kOutput, calls=%fused_computation.22 | convolution fusion | flops 2819948544 | bytes 7733252 | tf_op jit(solution)/shard_map/dot_general | solution.py:29
  65.1 4.4 fusion.11
  69.5 37.4 %all-gather.6.cloned.1.call-done = bf16[1536,1024]{1,0:T(8,128)(2,1)} async-done(((bf16[96,1024]{1,0:T(8,128)(2,1)}), bf16[1536,1024]{1,0:T(8,128)(2,1)}) %all-gather.6.cloned.1.call-update) | async-done | bytes 3145744 | tf_op jit(solution)/shard_map/all_gather | solution.py:27
  106.9 7.0 %fusion.10 = bf16[1536,896]{0,1:T(8,128)(2,1)} fusion(bf16[1536,1024]{1,0:T(8,128)(2,1)} %all-gather.6.cloned.1.call-done, bf16[1792,1024]{1,0:T(8,128)(2,1)} %param.9, s32[]{:T(128)S(6)} %select_n.2), kind=kOutput, calls=%fused_computation.20 | convolution fusion | flops 2819948544 | bytes 7733252 | tf_op jit(solution)/shard_map/dot_general | solution.py:31
  113.9 0.0 all-reduce.3.cloned.1.call-update
  113.9 0.0 all-gather.14.cloned.1.call-start
  114.0 103.0 %all-reduce.3.cloned.1.call-done = (bf16[1536,896]{0,1:T(8,128)(2,1)}, bf16[1536,896]{0,1:T(8,128)(2,1)}, bf16[1536,896]{0,1:T(8,128)(2,1)}) async-done(((bf16[1536,896]{0,1:T(8,128)(2,1)}, bf16[1536,896]{0,1:T(8,128)(2,1)}, bf16[1536,896]{0,1:T(8,128)(2,1)}), (bf16[1536,896]{0,1:T(8,128)(2,1)}, bf16[1536,896]{0,1:T(8,128)(2,1)}, bf16[1536,896]{0,1:T(8,128)(2,1)})) %all-reduce.3.cloned.1.call-update) | async-done | bytes 8257552 | tf_op jit(solution)/shard_map/psum | solution.py:36
  217.0 8.3 %fusion.16 = bf16[896,1024]{1,0:T(8,128)(2,1)} fusion(bf16[1536,1024]{1,0:T(8,128)(2,1)} %all-gather.6.cloned.1.call-done, bf16[1536,896]{0,1:T(8,128)(2,1)} %get-tuple-element.8, bf16[1536,896]{0,1:T(8,128)(2,1)} %get-tuple-element.10), kind=kOutput, calls=%fused_computation.27 | convolution fusion | flops 2830499840 | bytes 10485760 | tf_op jit(solution)/shard_map/dot_general | solution.py:46
  225.3 0.2 all-gather.12.cloned.1.call-start
  225.6 7.3 %convert_bitcast_fusion = bf16[1024,896]{0,1:T(8,128)(2,1)} fusion(bf16[1536,1024]{1,0:T(8,128)(2,1)} %all-gather.8.cloned.1.call-done, bf16[1536,896]{0,1:T(8,128)(2,1)} %get-tuple-element.10, bf16[1536,896]{0,1:T(8,128)(2,1)S(1)} %copy-done), kind=kOutput, calls=%fused_computation.24 | convolution fusion | flops 2830499840 | bytes 10485760 | tf_op jit(solution)/shard_map/dot_general | solution.py:43
  232.9 0.0 all-gather.10.cloned.1.call-start
  232.9 4.4 fusion.2
  237.3 1.5 copy-done.2
  238.9 4.1 convert_bitcast_fusion.1
  243.0 0.0 all-gather.10.cloned.1.call-update
  243.0 0.0 reduce-scatter.2.cloned.1.call-start
  243.1 6.0 %fusion.19 = f32[1536,1024]{1,0:T(8,128)S(1)} fusion(bf16[1536,896]{0,1:T(8,128)(2,1)} %copy-done.2, bf16[1024,1792]{1,0:T(8,128)(2,1)} %param.7, s32[]{:T(128)S(6)} %select_n.2), kind=kOutput, calls=%fused_computation.28 | convolution fusion | flops 2818572288 | bytes 10878980 | tf_op jit(solution)/shard_map/dot_general | solution.py:51
  249.1 5.2 %add_convert_fusion = bf16[1536,1024]{1,0:T(8,128)(2,1)} fusion(f32[1536,1024]{1,0:T(8,128)S(1)} %fusion.19, bf16[1024,1792]{1,0:T(8,128)(2,1)S(1)} %copy-done.4, s32[]{:T(128)S(6)} %select_n.2, bf16[1536,896]{0,1:T(8,128)(2,1)S(1)} %copy-done.1, bf16[1536,896]{0,1:T(8,128)(2,1)S(1)} %copy-done), kind=kOutput, calls=%fused_computation.6 | convolution fusion | flops 2832728064 | bytes 16777220 | tf_op jit(solution)/shard_map/dot_general | solution.py:54
  254.3 0.0 reduce-scatter.2.cloned.1.call-update
  254.3 26.8 %all-gather.14.cloned.1.call-done = bf16[1792,1024]{1,0:T(8,128)(2,1)} async-done(((bf16[896,1024]{1,0:T(8,128)(2,1)}), bf16[1792,1024]{1,0:T(8,128)(2,1)}) %all-gather.14.cloned.1.call-update) | async-done | bytes 3670032 | tf_op jit(solution)/shard_map/all_gather | solution.py:66
  281.1 56.5 %all-gather.12.cloned.1.call-done = bf16[1024,1792]{0,1:T(8,128)(2,1)} async-done(((bf16[1024,896]{0,1:T(8,128)(2,1)}), bf16[1024,1792]{0,1:T(8,128)(2,1)}) %all-gather.12.cloned.1.call-update) | async-done | bytes 3670032 | tf_op jit(solution)/shard_map/all_gather | solution.py:65
  337.6 5.9 %copy.10 = bf16[1024,1792]{1,0:T(8,128)(2,1)} copy(bf16[1024,1792]{0,1:T(8,128)(2,1)} %all-gather.12.cloned.1.call-done) | data formatting | bytes 7340032
  343.5 50.6 %all-gather.10.cloned.1.call-done = bf16[1024,1792]{0,1:T(8,128)(2,1)} async-done(((bf16[1024,896]{0,1:T(8,128)(2,1)}), bf16[1024,1792]{0,1:T(8,128)(2,1)}) %all-gather.10.cloned.1.call-update) | async-done | bytes 3670032 | tf_op jit(solution)/shard_map/all_gather | solution.py:64
  394.1 5.9 %copy.9 = bf16[1024,1792]{1,0:T(8,128)(2,1)} copy(bf16[1024,1792]{0,1:T(8,128)(2,1)} %all-gather.10.cloned.1.call-done) | data formatting | bytes 7340032
  400.0 71.1 %reduce-scatter.2.cloned.1.call-done = bf16[96,1024]{1,0:T(8,128)(2,1)} async-done(((bf16[1536,1024]{1,0:T(8,128)(2,1)}), bf16[96,1024]{1,0:T(8,128)(2,1)}) %reduce-scatter.2.cloned.1.call-update) | async-done | bytes 196624 | tf_op jit(solution)/shard_map/reduce_scatter | solution.py:49
  471.2 4.2 copy.15
  (15 shorter events, 0.1 us)
Async XLA Ops:
  7.2 50.7 %all-gather.8.cloned.1.call-start = ((), (), s32[]{:S(2)}) async-start(), calls=%async_computation.2 | async-start | bytes 3342336 | tf_op jit(solution)/shard_map/all_gather | solution.py:26
  7.9 99.0 %all-gather.6.cloned.1.call-start = ((), (), s32[]{:S(2)}) async-start(), calls=%async_computation.1 | async-start | bytes 3342336 | tf_op jit(solution)/shard_map/all_gather | solution.py:27
  8.6 208.4 %all-reduce.3.cloned.1.call-start = ((), (), s32[]{:S(2)}) async-start(), calls=%async_computation.7 | async-start | bytes 16515072 | tf_op jit(solution)/shard_map/psum | solution.py:36
  57.9 7.2 %copy-start.3 = (bf16[1024,1792]{1,0:T(8,128)(2,1)S(1)}, bf16[1024,1792]{1,0:T(8,128)(2,1)}, u32[]{:S(2)}) copy-start(bf16[1024,1792]{1,0:T(8,128)(2,1)} %param.8) | copy-start | bytes 11010052
  57.9 7.2 %copy-start.5 = (bf16[1536,1024]{1,0:T(8,128)(2,1)S(1)}, bf16[1536,1024]{1,0:T(8,128)(2,1)}, u32[]{:S(2)}) copy-start(bf16[1536,1024]{1,0:T(8,128)(2,1)} %all-gather.8.cloned.1.call-done) | copy-start | bytes 9437188
  113.9 167.2 %all-gather.14.cloned.1.call-start = ((), (), s32[]{:S(2)}) async-start(), calls=%async_computation.6 | async-start | bytes 5505024 | tf_op jit(solution)/shard_map/all_gather | solution.py:66
  217.0 8.5 %copy-start = (bf16[1536,896]{0,1:T(8,128)(2,1)S(1)}, bf16[1536,896]{0,1:T(8,128)(2,1)}, u32[]{:S(2)}) copy-start(bf16[1536,896]{0,1:T(8,128)(2,1)} %get-tuple-element.9) | copy-start | bytes 8257540
  225.3 112.3 %all-gather.12.cloned.1.call-start = ((), (), s32[]{:S(2)}) async-start(), calls=%async_computation.5 | async-start | bytes 5505024 | tf_op jit(solution)/shard_map/all_gather | solution.py:65
  232.9 161.3 %all-gather.10.cloned.1.call-start = ((), (), s32[]{:S(2)}) async-start(), calls=%async_computation.4 | async-start | bytes 5505024 | tf_op jit(solution)/shard_map/all_gather | solution.py:64
  232.9 6.0 %copy-start.6 = (bf16[1536,1024]{1,0:T(8,128)(2,1)S(1)}, bf16[1536,1024]{1,0:T(8,128)(2,1)}, u32[]{:S(2)}) copy-start(bf16[1536,1024]{1,0:T(8,128)(2,1)} %all-gather.8.cloned.1.call-done) | copy-start | bytes 9437188
  237.3 1.5 copy-start.2
  243.0 228.2 %reduce-scatter.2.cloned.1.call-start = ((), (), s32[]{:S(2)}) async-start(), calls=%async_computation.3 | async-start | bytes 3342336 | tf_op jit(solution)/shard_map/reduce_scatter | solution.py:49
  243.1 6.0 %copy-start.1 = (bf16[1536,896]{0,1:T(8,128)(2,1)S(1)}, bf16[1536,896]{0,1:T(8,128)(2,1)}, u32[]{:S(2)}) copy-start(bf16[1536,896]{0,1:T(8,128)(2,1)} %get-tuple-element.10) | copy-start | bytes 8257540
  243.1 6.0 %copy-start.4 = (bf16[1024,1792]{1,0:T(8,128)(2,1)S(1)}, bf16[1024,1792]{1,0:T(8,128)(2,1)}, u32[]{:S(2)}) copy-start(bf16[1024,1792]{1,0:T(8,128)(2,1)} %param.8) | copy-start | bytes 11010052
Sparse Core Ops, SparseCore 0:
  10.2 47.6 all-gather.7
  60.1 46.7 all-gather.5
  114.1 102.9 all-reduce.2
  225.4 55.6 all-gather.13
  283.3 54.2 all-gather.11
  339.8 54.2 all-gather.9
  398.4 72.7 reduce-scatter.1
where the time goes:
time: 486 us; the launch traced here: 482 us
  waiting for transfers between devices  396 us (81%)
  matrix products  49.4 us (10%)
  local copies, waits for them, and re-layouts  17.6 us (4%)
  between operations  14.2 us (3%)
    psum x1, waiting for transfers between devices, per_device(): lax.psum(up_part.astype(jnp.bfloat16), 'row').astype(jnp.float32)  103 us
    reduce_scatter x1, waiting for transfers between devices, per_device(): lax.psum_scatter((lax.dot_general(grad_gate_act, gate_cols, contract_last...  71.1 us
    all_gather x1, waiting for transfers between devices, per_device(): lax.all_gather(up_half.astype(jnp.bfloat16), 'depth', axis=1, tiled=True)  56.5 us
    all_gather x1, waiting for transfers between devices, per_device(): lax.all_gather(gate_half.astype(jnp.bfloat16), 'depth', axis=1, tiled=True)  50.6 us
    all_gather x1, waiting for transfers between devices, per_device(): lax.all_gather(inputs, ('depth', 'col'), axis=0, tiled=True)  49.2 us
    all_gather x1, waiting for transfers between devices, per_device(): lax.all_gather(grad_out, ('depth', 'col'), axis=0, tiled=True)  37.4 us
    all_gather x1, waiting for transfers between devices, per_device(): lax.all_gather(down_half.astype(jnp.bfloat16), 'depth', axis=0, tiled=True)  26.8 us
    unnamed x17, local copies, waits for them, and re-layouts  17.6 us
  transfers between devices with their start and end apart: 7, of which 7 were waited for; matrix products, arithmetic and copies ran while one was open for 10% of the time, Pallas kernels for 0%

commit v1 on v0

v1 whole, which is shorter than its diff:
```python
import functools

import jax
import jax.numpy as jnp
from jax import lax
from jax.experimental import pallas as pl
from jax.experimental.pallas import tpu as pltpu
from jax.sharding import PartitionSpec as P

MESH = pl.DeviceIdType.MESH
BF16, F32 = jnp.bfloat16, jnp.float32
BLOCK = 96
CHUNK = 192
PIECE = 48
NCHUNK = 4
WIDTH = 1024
HID = 1792
HALF = 896
Y_OFFSET = (0, 1, 3, 2)
TRANS = (((1,), (1,)), ((), ()))


def multiple(value, of):
    return pl.multiple_of(value, of)


def names():
    out = ["g_xl", "g_xo", "g_x2"]
    out += [f"gy_{way}_{what}" for way in "mp2" for what in ("own", "par", "oth")]
    for j in range(NCHUNK):
        out += [f"{n}{j}" for n in (
            "core", "relA", "relB", "finA", "finB",
            "agA", "agB", "agA2", "agB2", "agX", "agXh",
            "ogA", "ogB", "ogA2", "ogB2",
            "cOwn", "cB", "cA", "cA2", "cB2",
            "oOwn", "oB", "oA", "oA2", "oB2", "oH",
            "giS", "giO",
        )]
    return {n: i for i, n in enumerate(out)}


NAMES = names()
N_FLUSH = 8 * 6 + 2


def kernel(x_in, g_in, gw_in, uw_in, dw_in,
           gin_out, x_out, g_out, a0_out, a1_out, a2_out,
           gw, uw, dw, xg, act, core_send, core_recv, part, relay, final, gi_send, gi_recv,
           send_sems, recv_sems, load_sems, flush_sems):
    d, r, c = lax.axis_index("depth"), lax.axis_index("row"), lax.axis_index("col")
    z, k = r // 2, r % 2
    xl, y = c // 4, c % 4
    za = (z + 1 + 2 * k) % 4
    zb = (z + 3 - 2 * k) % 4
    z2 = (z + 2) % 4
    core = (d, r + 1 - 2 * k, c)
    to_a, to_b = (d, za * 2 + k, c), (d, zb * 2 + k, c)
    y_m, y_p, y_2 = (y + 3) % 4, (y + 1) % 4, (y + 2) % 4
    y_dev = {"m": (d, r, xl * 4 + y_m), "p": (d, r, xl * 4 + y_p), "2": (d, r, xl * 4 + y_2)}
    diag = [(d, r, (1 - xl) * 4 + v) for v in (y_m, y_p, y_2)]
    to_xl = (d, r, (1 - xl) * 4 + y)
    to_xo = (1 - d, r, (1 - xl) * 4 + y)
    to_x2 = (1 - d, r, c)
    everyone = [core, to_a, to_b, *y_dev.values(), *diag, to_xl, to_xo, to_x2]

    started = []

    def send(name, src, dst, device):
        i = NAMES[name]
        copy = pltpu.make_async_remote_copy(
            src_ref=src, dst_ref=dst, send_sem=send_sems.at[i], recv_sem=recv_sems.at[i],
            device_id=device, device_id_type=MESH)
        copy.start()
        started.append(copy)

    def arrived(name, dst):
        i = NAMES[name]
        pltpu.make_async_remote_copy(
            src_ref=dst, dst_ref=dst, send_sem=send_sems.at[i], recv_sem=recv_sems.at[i],
            device_id=core, device_id_type=MESH).wait_recv()

    own_rows = pl.ds(multiple(xl * BLOCK, BLOCK), BLOCK)
    par_rows = pl.ds(multiple((1 - xl) * BLOCK, BLOCK), BLOCK)
    loads = [
        pltpu.make_async_copy(x_in, xg.at[0, 0, own_rows], load_sems.at[0]),
        pltpu.make_async_copy(g_in, xg.at[1, 0, own_rows], load_sems.at[1]),
        pltpu.make_async_copy(gw_in, gw, load_sems.at[2]),
        pltpu.make_async_copy(uw_in, uw, load_sems.at[3]),
        pltpu.make_async_copy(dw_in, dw, load_sems.at[4]),
    ]
    for load in loads:
        load.start()

    barrier = pltpu.get_barrier_semaphore()
    for device in everyone:
        pl.semaphore_signal(barrier, inc=1, device_id=device, device_id_type=MESH)
    pl.semaphore_wait(barrier, len(everyone))

    loads[0].wait()
    loads[1].wait()
    own = xg.at[:, 0, own_rows]
    par = xg.at[:, 0, par_rows]
    ARRIVE = {"m": 1, "p": 2, "2": 3}
    send("g_xl", own, own, to_xl)
    send("gy_m_own", own, xg.at[:, 1, own_rows], y_dev["m"])
    send("gy_p_own", own, xg.at[:, 2, own_rows], y_dev["p"])

    def gather_two():
        arrived("g_xl", par)
        send("gy_m_par", par, xg.at[:, 1, par_rows], y_dev["m"])
        send("gy_p_par", par, xg.at[:, 2, par_rows], y_dev["p"])
        send("g_xo", own, xg.at[:, 4, own_rows], to_xo)
        send("g_x2", own, xg.at[:, 4, own_rows], to_x2)

    def gather_three():
        send("gy_2_own", own, xg.at[:, 3, own_rows], y_dev["2"])
        send("gy_2_par", par, xg.at[:, 3, par_rows], y_dev["2"])

    def gather_four():
        arrived("g_x2", xg.at[:, 4, own_rows])
        arrived("g_xo", xg.at[:, 4, par_rows])
        for way in "mp2":
            send(f"gy_{way}_oth", xg.at[:, 4], xg.at[:, 4 + ARRIVE[way]], y_dev[way])

    def gathered(way):
        arrived(f"gy_{way}_own", xg.at[:, ARRIVE[way], own_rows])
        arrived(f"gy_{way}_par", xg.at[:, ARRIVE[way], par_rows])

    cols_own = pl.ds(multiple(k * HALF, 128), HALF)
    cols_par = pl.ds(multiple((1 - k) * HALF, 128), HALF)

    def products(j, cols, rows, out):
        x, g = xg[0, j], xg[1, j]
        out[0] = jnp.dot(x, gw[:, cols], preferred_element_type=F32).astype(BF16)
        out[1] = jnp.dot(x, uw[:, cols], preferred_element_type=F32).astype(BF16)
        out[2] = lax.dot_general(g, dw[rows, :], TRANS, preferred_element_type=F32).astype(BF16)

    def piece(zz):
        return pl.ds(multiple(zz * PIECE, 16), PIECE)

    p_own, p_a, p_b, p_2 = piece(z), piece(za), piece(zb), piece(z2)

    def forward(j):
        products(j, cols_par, cols_par, core_send.at[j])
        send(f"core{j}", core_send.at[j], core_recv.at[j], core)
        products(j, cols_own, cols_own, part.at[j])

    def add_core(j):
        arrived(f"core{j}", core_recv.at[j])

        def add(rows):
            part[j, :, rows] = (part[j, :, rows].astype(F32) + core_recv[j, :, rows].astype(F32)).astype(BF16)

        add(p_2)
        send(f"relA{j}", part.at[j, pl.ds(0, 2), p_2], relay.at[j, pl.ds(0, 2)], to_a)
        send(f"relB{j}", part.at[j, pl.ds(2, 1), p_2], relay.at[j, pl.ds(2, 1)], to_b)
        add(p_a)
        add(p_b)
        add(p_own)

    def add_relay(j):
        arrived(f"relA{j}", relay.at[j, pl.ds(0, 2)])
        part[j, 0:2, p_a] = (part[j, 0:2, p_a].astype(F32) + relay[j, 0:2].astype(F32)).astype(BF16)
        send(f"finA{j}", part.at[j, :, p_a], final.at[j, 0], to_a)
        arrived(f"relB{j}", relay.at[j, pl.ds(2, 1)])
        part[j, 2:3, p_b] = (part[j, 2:3, p_b].astype(F32) + relay[j, 2:3].astype(F32)).astype(BF16)
        send(f"finB{j}", part.at[j, :, p_b], final.at[j, 1], to_b)

    def activations(j):
        arrived(f"finA{j}", final.at[j, 0])
        arrived(f"finB{j}", final.at[j, 1])
        gate, up, grad = (
            part[j, t, p_own].astype(F32) + final[j, 0, t].astype(F32) + final[j, 1, t].astype(F32)
            for t in range(3))
        sig = jax.nn.sigmoid(gate)
        act[0, k, j, p_own] = (grad * up * sig * (1.0 + gate * (1.0 - sig))).astype(BF16)
        act[1, k, j, p_own] = (grad * gate * sig).astype(BF16)
        act[2, k, j, p_own] = (gate * sig * up).astype(BF16)
        mine = act.at[:, k, j, p_own]
        send(f"agA{j}", mine, mine, to_a)
        send(f"agB{j}", mine, mine, to_b)
        send(f"agX{j}", act.at[pl.ds(0, 2), k, j, p_own], act.at[pl.ds(0, 2), k, 4 + j, p_own], to_x2)
        send(f"cOwn{j}", mine, mine, core)

    def block(t, n, kk, pj, rows):
        return act.at[pl.ds(t, n), kk, pj, rows]

    def pass_on(name, ref, device):
        send(name, ref, ref, device)

    def spread_own(j):
        arrived(f"agA{j}", block(0, 3, k, j, p_b))
        pass_on(f"agA2{j}", block(0, 2, k, j, p_b), to_a)
        pass_on(f"cB{j}", block(0, 3, k, j, p_b), core)
        arrived(f"agB{j}", block(0, 3, k, j, p_a))
        pass_on(f"agB2{j}", block(2, 1, k, j, p_a), to_b)
        pass_on(f"cA{j}", block(0, 3, k, j, p_a), core)

    def spread_other(j):
        mine = block(0, 2, k, 4 + j, p_own)
        arrived(f"agX{j}", mine)
        pass_on(f"ogA{j}", mine, to_a)
        pass_on(f"ogB{j}", mine, to_b)
        pass_on(f"oOwn{j}", mine, core)

    def end_own(j):
        arrived(f"agA2{j}", block(0, 2, k, j, p_2))
        pass_on(f"cA2{j}", block(0, 2, k, j, p_2), core)
        arrived(f"agB2{j}", block(2, 1, k, j, p_2))
        pass_on(f"cB2{j}", block(2, 1, k, j, p_2), core)
        send(f"agXh{j}", act.at[2, k, j], act.at[2, k, 4 + j], to_x2)

    def relay_other(j):
        arrived(f"ogA{j}", block(0, 2, k, 4 + j, p_b))
        pass_on(f"ogA2{j}", block(0, 1, k, 4 + j, p_b), to_a)
        pass_on(f"oB{j}", block(0, 2, k, 4 + j, p_b), core)
        arrived(f"ogB{j}", block(0, 2, k, 4 + j, p_a))
        pass_on(f"ogB2{j}", block(1, 1, k, 4 + j, p_a), to_b)
        pass_on(f"oA{j}", block(0, 2, k, 4 + j, p_a), core)

    def end_other(j):
        arrived(f"ogA2{j}", block(0, 1, k, 4 + j, p_2))
        pass_on(f"oA2{j}", block(0, 1, k, 4 + j, p_2), core)
        arrived(f"ogB2{j}", block(1, 1, k, 4 + j, p_2))
        pass_on(f"oB2{j}", block(1, 1, k, 4 + j, p_2), core)
        arrived(f"agXh{j}", act.at[2, k, 4 + j])
        pass_on(f"oH{j}", act.at[2, k, 4 + j], core)

    flushes = []

    def flush(src, dst):
        copy = pltpu.make_async_copy(src, dst, flush_sems.at[len(flushes)])
        copy.start()
        flushes.append(copy)

    def flush_act(pj):
        for t, out in enumerate((a0_out, a1_out, a2_out)):
            for kk in range(2):
                flush(act.at[t, kk, pj], out.at[pj, :, pl.ds(kk * HALF, HALF)])

    def input_grad(j):
        kp = 1 - k
        arrived(f"cOwn{j}", block(0, 3, kp, j, p_own))
        arrived(f"cB{j}", block(0, 3, kp, j, p_b if False else piece((z + 3 - 2 * kp) % 4)))
        arrived(f"cA{j}", block(0, 3, kp, j, piece((z + 1 + 2 * kp) % 4)))
        arrived(f"cA2{j}", block(0, 2, kp, j, p_2))
        arrived(f"cB2{j}", block(2, 1, kp, j, p_2))
        total = None
        for t, w in enumerate((gw, uw)):
            for kk in range(2):
                term = lax.dot_general(act[t, kk, j], w[:, kk * HALF:(kk + 1) * HALF], TRANS,
                                       preferred_element_type=F32)
                total = term if total is None else total + term
        gi_send[j] = total.astype(BF16)
        yy = (y + Y_OFFSET[j]) % 4
        if j:
            send(f"giS{j}", gi_send.at[j, own_rows], gi_recv.at[2 * j], (d, r, xl * 4 + yy))
        send(f"giO{j}", gi_send.at[j, par_rows], gi_recv.at[2 * j + 1], (d, r, (1 - xl) * 4 + yy))
        flush_act(j)

    def flush_other(j):
        kp = 1 - k
        arrived(f"oOwn{j}", block(0, 2, kp, 4 + j, p_own))
        arrived(f"oB{j}", block(0, 2, kp, 4 + j, piece((z + 3 - 2 * kp) % 4)))
        arrived(f"oA{j}", block(0, 2, kp, 4 + j, piece((z + 1 + 2 * kp) % 4)))
        arrived(f"oA2{j}", block(0, 1, kp, 4 + j, p_2))
        arrived(f"oB2{j}", block(1, 1, kp, 4 + j, p_2))
        arrived(f"oH{j}", act.at[2, kp, 4 + j])
        flush_act(4 + j)

    def flush_tokens():
        for way in "mp2":
            arrived(f"gy_{way}_oth", xg.at[:, 4 + ARRIVE[way]])
        flush(xg.at[0], x_out)
        flush(xg.at[1], g_out)

    gather_two()
    for load in loads[2:]:
        load.wait()
    forward(0)
    gather_three()
    add_core(0)
    gathered("m")
    forward(1)
    add_relay(0)
    add_core(1)
    gather_four()
    activations(0)
    add_relay(1)
    spread_own(0)
    spread_other(0)
    gathered("p")
    forward(2)
    add_core(2)
    activations(1)
    end_own(0)
    add_relay(2)
    relay_other(0)
    spread_own(1)
    spread_other(1)
    gathered("2")
    forward(3)
    add_core(3)
    end_other(0)
    input_grad(0)
    activations(2)
    end_own(1)
    add_relay(3)
    relay_other(1)
    spread_own(2)
    spread_other(2)
    end_other(1)
    input_grad(1)
    flush_other(0)
    activations(3)
    end_own(2)
    relay_other(2)
    spread_own(3)
    spread_other(3)
    flush_tokens()
    end_other(2)
    input_grad(2)
    flush_other(1)
    end_own(3)
    relay_other(3)
    input_grad(3)
    flush_other(2)
    end_other(3)
    flush_other(3)

    total = gi_send[0, own_rows].astype(F32)
    for j in range(NCHUNK):
        if j:
            arrived(f"giS{j}", gi_recv.at[2 * j])
            total = total + gi_recv[2 * j].astype(F32)
        arrived(f"giO{j}", gi_recv.at[2 * j + 1])
        total = total + gi_recv[2 * j + 1].astype(F32)
    gin_out[...] = total.astype(BF16)
    for copy in started:
        copy.wait_send()
    for copy in flushes:
        copy.wait()


def per_device(inputs, grad_out, gate_weight, up_weight, down_weight):
    over_tokens = (((0,), (0,)), ((), ()))
    hbm = pl.BlockSpec(memory_space=pl.ANY)
    n = len(NAMES)
    grad_in, x, g, gate_act, up_act, hidden = pl.pallas_call(
        kernel,
        out_shape=(
            jax.ShapeDtypeStruct((BLOCK, WIDTH), BF16),
            jax.ShapeDtypeStruct((8, CHUNK, WIDTH), BF16),
            jax.ShapeDtypeStruct((8, CHUNK, WIDTH), BF16),
            jax.ShapeDtypeStruct((8, CHUNK, HID), BF16),
            jax.ShapeDtypeStruct((8, CHUNK, HID), BF16),
            jax.ShapeDtypeStruct((8, CHUNK, HID), BF16),
        ),
        in_specs=[hbm] * 5,
        out_specs=(pl.BlockSpec(memory_space=pltpu.VMEM),) + (hbm,) * 5,
        scratch_shapes=[
            pltpu.VMEM((WIDTH, HID), BF16),
            pltpu.VMEM((WIDTH, HID), BF16),
            pltpu.VMEM((HID, WIDTH), BF16),
            pltpu.VMEM((2, 8, CHUNK, WIDTH), BF16),
            pltpu.VMEM((3, 2, 8, CHUNK, HALF), BF16),
            pltpu.VMEM((NCHUNK, 3, CHUNK, HALF), BF16),
            pltpu.VMEM((NCHUNK, 3, CHUNK, HALF), BF16),
            pltpu.VMEM((NCHUNK, 3, CHUNK, HALF), BF16),
            pltpu.VMEM((NCHUNK, 3, PIECE, HALF), BF16),
            pltpu.VMEM((NCHUNK, 2, 3, PIECE, HALF), BF16),
            pltpu.VMEM((NCHUNK, CHUNK, WIDTH), BF16),
            pltpu.VMEM((8, BLOCK, WIDTH), BF16),
            pltpu.SemaphoreType.DMA((n,)),
            pltpu.SemaphoreType.DMA((n,)),
            pltpu.SemaphoreType.DMA((5,)),
            pltpu.SemaphoreType.DMA((N_FLUSH,)),
        ],
        compiler_params=pltpu.CompilerParams(
            collective_id=0, has_side_effects=True, vmem_limit_bytes=62 * 2**20),
        name="ffn_exchange",
    )(inputs, grad_out, gate_weight, up_weight, down_weight)

    def weight_grad(a, b):
        a, b = (v.reshape(v.shape[0] * v.shape[1], v.shape[2]) for v in (a, b))
        return lax.dot_general(a, b, over_tokens, preferred_element_type=F32).astype(BF16)

    return grad_in, weight_grad(x, gate_act), weight_grad(x, up_act), weight_grad(hidden, g)


def solution(mesh):
    in_specs = (
        P(("depth", "col"), "row"),
        P(("depth", "col"), "row"),
        P("row", "col"),
        P("row", "col"),
        P("col", "row"),
    )
    out_specs = (P(("depth", "col"), "row"), P("row", "col"), P("row", "col"), P("col", "row"))
    return jax.shard_map(
        per_device, mesh=mesh, in_specs=in_specs, out_specs=out_specs, check_vma=False
    )
```

time: 486 us -> 167 us (0.34)
  waiting for transfers between devices: 396 us -> 0 us
  Pallas kernels: 0 us -> 140 us
  matrix products: 49.4 us -> 25.6 us
  local copies, waits for them, and re-layouts: 17.6 us -> 0.7 us
  between operations: 14.2 us -> 0.7 us
    all_gather x5 -> x0, waiting for transfers between devices: 221 us -> none  [the longest x1 56.5 us: per_device(): lax.all_gather(up_half.astype(jnp.bfloat16), 'depth', axis=1, tiled=True)]
    pallas_call x0 -> x1, Pallas kernels: none -> 140 us  [per_device(): pl.pallas_call(kernel, out_shape=(jax.ShapeDtypeStruct((BLOCK, WIDTH), BF...]
    psum x1 -> x0, waiting for transfers between devices: 103 us -> none  [per_device(): lax.psum(up_part.astype(jnp.bfloat16), 'row').astype(jnp.float32)]
    reduce_scatter x1 -> x0, waiting for transfers between devices: 71.1 us -> none  [per_device(): lax.psum_scatter((lax.dot_general(grad_gate_act, gate_cols, contract_last...]
    dot_general x8 -> x3, matrix products: 49.4 us -> 25.6 us  [weight_grad(): lax.dot_general(a, b, over_tokens, preferred_element_type=F32).astype(BF16)]
    unnamed x17 -> x13, local copies, waits for them, and re-layouts: 17.6 us -> 0.7 us
  transfers between devices with their start and end apart: 7 -> 0, of which waited for: 7 -> 0; matrix products, arithmetic and copies ran while one was open for 10% -> 0% of each run, Pallas kernels for 0% -> 0%
where the time goes in v1:
time: 167 us
  Pallas kernels  140 us (84%)
  matrix products  25.6 us (15%)
    pallas_call x1, Pallas kernels, per_device(): pl.pallas_call(kernel, out_shape=(jax.ShapeDtypeStruct((BLOCK, WIDTH), BF...  140 us
    dot_general x3, matrix products, weight_grad(): lax.dot_general(a, b, over_tokens, preferred_element_type=F32).astype(BF16)  25.6 us

profile of v1, /device:TPU:73, one launch (start us, length us, event | category | flops | bytes accessed | tf_op | source)
XLA Modules:
  0.0 167.1 jit_solution(6847468220656597230)
XLA Ops:
  0.6 140.1 %ffn_exchange.1 = (bf16[96,1024]{1,0:T(8,128)(2,1)}, bf16[8,192,1024]{2,1,0:T(8,128)(2,1)}, bf16[8,192,1024]{2,1,0:T(8,128)(2,1)}, bf16[8,192,1792]{2,1,0:T(8,12...) custom-call(bf16[96,1024]{1,0:T(8,128)(2,1)} %x_in.1, bf16[96,1024]{1,0:T(8,128)(2,1)} %g_in.1, ...), custom_call_target="tpu_custom_call" | custom-call | tf_op jit(solution)/shard_map/ffn_exchange/pallas_call | solution.py:349
  140.7 0.0 copy-start.1
  140.7 0.0 copy-start.3
  140.7 0.0 slice-start
  140.7 10.8 %bitcast_convert_fusion.2 = bf16[1024,1792]{1,0:T(8,128)(2,1)} fusion(bf16[8,192,1024]{2,1,0:T(8,128)(2,1)} %get-tuple-element.11, bf16[8,192,1792]{2,1,0:T(8,128)(2,1)} %get-tuple-element.12), kind=kOutput, calls=%fused_computation.2 | convolution fusion | flops 5638979584 | bytes 12320768 | tf_op jit(solution)/shard_map/dot_general | solution.py:386
  151.5 0.0 copy-done.1
  151.5 0.0 copy-done.3
  151.5 0.0 slice-start.1
  151.5 0.0 copy-start.2
  151.5 7.5 %bitcast_convert_fusion.1 = bf16[1024,1792]{1,0:T(8,128)(2,1)} fusion(bf16[8,192,1024]{2,1,0:T(8,128)(2,1)S(1)} %copy-done.3, bf16[8,192,1792]{2,1,0:T(8,128)(2,1)S(1)} %copy-done.1), kind=kOutput, calls=%fused_computation.1 | convolution fusion | flops 5638979584 | bytes 12320768 | tf_op jit(solution)/shard_map/dot_general | solution.py:386
  159.0 0.0 slice-done
  159.0 0.0 slice-done.1
  159.0 0.0 copy-done.2
  159.0 0.0 copy-start
  159.0 7.4 %bitcast_convert_fusion = bf16[1792,1024]{1,0:T(8,128)(2,1)} fusion(bf16[8,192,1792]{2,1,0:T(8,128)(2,1)S(1)} %bitcast.13, bf16[8,192,1024]{2,1,0:T(8,128)(2,1)S(1)} %copy-done.2), kind=kOutput, calls=%fused_computation | convolution fusion | flops 5638979584 | bytes 12320768 | tf_op jit(solution)/shard_map/dot_general | solution.py:386
  166.4 0.0 copy-done
  166.4 0.7 copy.10
  (1 shorter events, 0.0 us)
Async XLA Ops:
  140.7 10.8 %copy-start.1 = (bf16[8,192,1792]{2,1,0:T(8,128)(2,1)S(1)}, bf16[8,192,1792]{2,1,0:T(8,128)(2,1)}, u32[]{:S(2)}) copy-start(bf16[8,192,1792]{2,1,0:T(8,128)(2,1)} %get-tuple-element.13) | copy-start | bytes 16515076
  140.7 10.8 %copy-start.3 = (bf16[8,192,1024]{2,1,0:T(8,128)(2,1)S(1)}, bf16[8,192,1024]{2,1,0:T(8,128)(2,1)}, u32[]{:S(2)}) copy-start(bf16[8,192,1024]{2,1,0:T(8,128)(2,1)} %get-tuple-element.11) | copy-start | bytes 9437188
  140.7 18.3 %slice-start = ((s8[5505024]{0:T(1024)(128)(4,1)}), s8[4194304]{0:T(1024)(128)(4,1)S(1)}, s32[]{:S(2)}) async-start(s8[5505024]{0:T(1024)(128)(4,1)} %bitcast.12), calls=%async_computation | async-start | bytes 8388608
  151.5 7.5 %slice-start.1 = ((s8[5505024]{0:T(1024)(128)(4,1)}), s8[1310720]{0:T(1024)(128)(4,1)S(1)}, s32[]{:S(2)}) async-start(s8[5505024]{0:T(1024)(128)(4,1)} %bitcast.12), calls=%async_computation.1 | async-start | bytes 2621440
  151.5 7.5 %copy-start.2 = (bf16[8,192,1024]{2,1,0:T(8,128)(2,1)S(1)}, bf16[8,192,1024]{2,1,0:T(8,128)(2,1)}, u32[]{:S(2)}) copy-start(bf16[8,192,1024]{2,1,0:T(8,128)(2,1)} %get-tuple-element.15) | copy-start | bytes 9437188
  159.0 7.4 %copy-start = (bf16[96,1024]{1,0:T(8,128)(2,1)S(1)}, bf16[96,1024]{1,0:T(8,128)(2,1)}, u32[]{:S(2)}) copy-start(bf16[96,1024]{1,0:T(8,128)(2,1)} %get-tuple-element.20) | copy-start | bytes 589828

commit v2 on v0

v2 whole, which is shorter than its diff:
```python
import jax
import jax.numpy as jnp
from jax import lax
from jax.experimental import pallas as pl
from jax.experimental.pallas import tpu as pltpu
from jax.sharding import PartitionSpec as P

MESH = pl.DeviceIdType.MESH
BF16, F32 = jnp.bfloat16, jnp.float32
BLOCK = 96
PLANE = 768
EARLY = 384
WIDTH = 1024
HID = 1792
HALF = 896
TRANS = (((1,), (1,)), ((), ()))
OVER_TOKENS = (((0,), (0,)), ((), ()))
OWN, PAR, M0, Q0, M1, Q1, T0, T1 = range(8)
CHUNKS = (192, 192, 192, 192)
BASE = tuple(sum(CHUNKS[:i]) for i in range(len(CHUNKS) + 1))
GI_GROUPS = ((OWN, PAR), (M0, Q0), (M1, Q1), (T0, T1))
ORDER = (
    ("G4",), ("G2",), ("F", 0), ("G3",), ("P", 0), ("F", 1), ("R", 0), ("P", 1), ("G5",), ("C", 0), ("R", 1),
    ("D1", 0), ("D2", 0), ("F", 2), ("P", 2), ("C", 1), ("D3", 0), ("R", 2), ("D4", 0), ("D1", 1), ("D2", 1),
    ("F", 3), ("P", 3), ("D5", 0), ("D6", 0), ("E", 0), ("C", 2), ("D3", 1), ("R", 3), ("D4", 1), ("D1", 2),
    ("D2", 2), ("D5", 1), ("D6", 1), ("E", 1), ("H", 0), ("C", 3), ("D3", 2), ("D4", 2), ("D1", 3), ("D2", 3),
    ("GF",), ("D5", 2), ("D6", 2), ("E", 2), ("H", 1), ("W", 0, 0), ("W", 0, 1), ("D3", 3), ("W", 0, 2),
    ("W", 0, 3), ("W", 1, 0), ("D4", 3), ("W", 1, 1), ("W", 1, 2), ("W", 1, 3), ("V", 0, 0), ("E", 3),
    ("V", 0, 1), ("V", 0, 2), ("V", 0, 3), ("H", 2), ("D5", 3), ("V", 1, 0), ("V", 1, 1), ("D6", 3),
    ("V", 1, 2), ("V", 1, 3), ("H", 3),
)
STEPS = (
    "core", "relA", "relB", "finA", "finB", "agA", "agB", "agA2", "agB2", "agX", "agXh",
    "ogA", "ogB", "ogA2", "ogB2", "cOwn", "cB", "cA", "cA2", "cB2", "oOwn", "oB", "oA", "oA2", "oB2", "oH",
)


def names():
    out = ["g_xl", "g_xo", "g_x2"]
    out += [f"gy_{way}_{what}" for way in "mp2" for what in ("own", "par", "oth0", "oth1")]
    out += [f"gi{b}" for b in range(1, 8)]
    for j in range(len(CHUNKS)):
        out += [f"{n}{j}" for n in STEPS]
    return {n: i for i, n in enumerate(out)}


NAMES = names()
N_FLUSH = 2 * len(CHUNKS) * 6 + 2


def multiple(value, of):
    return pl.multiple_of(value, of)


def rows_of(block, count=1):
    return pl.ds(block * BLOCK, count * BLOCK)


def place(plane, row):
    return plane * EARLY + row + (EARLY if row >= EARLY else 0)


def kernel(x_in, g_in, gw_in, uw_in, dw_in,
           gin_out, x_out, g_out, a0_out, a1_out, a2_out, p0_out, p1_out, p2_out,
           gw, uw, dw, xg, act, core_send, core_recv, part, relay, final, gi_send, gi_recv, wg,
           send_sems, recv_sems, load_sems, flush_sems, wg_sems):
    d, r, c = lax.axis_index("depth"), lax.axis_index("row"), lax.axis_index("col")
    z, k = r // 2, r % 2
    kp = 1 - k
    xl, y = c // 4, c % 4
    za = (z + 1 + 2 * k) % 4
    zb = (z + 3 - 2 * k) % 4
    z2 = (z + 2) % 4
    core = (d, r + 1 - 2 * k, c)
    to_a, to_b = (d, za * 2 + k, c), (d, zb * 2 + k, c)
    y_m, y_p, y_2 = (y + 3) % 4, (y + 1) % 4, (y + 2) % 4
    same = {w: (d, r, xl * 4 + v) for w, v in (("m", y_m), ("p", y_p), ("2", y_2))}
    diag = {w: (d, r, (1 - xl) * 4 + v) for w, v in (("m", y_m), ("p", y_p), ("2", y_2))}
    to_xl = (d, r, (1 - xl) * 4 + y)
    to_xo = (1 - d, r, (1 - xl) * 4 + y)
    to_x2 = (1 - d, r, c)
    everyone = [core, to_a, to_b, *same.values(), *diag.values(), to_xl, to_xo, to_x2]
    at_own = {"m": Q0, "p": M0, "2": T0}
    at_par = {"m": Q1, "p": M1, "2": T1}

    started = []

    def send(name, src, dst, device):
        i = NAMES[name]
        copy = pltpu.make_async_remote_copy(
            src_ref=src, dst_ref=dst, send_sem=send_sems.at[i], recv_sem=recv_sems.at[i],
            device_id=device, device_id_type=MESH)
        copy.start()
        started.append(copy)

    def arrived(name, dst):
        i = NAMES[name]
        pltpu.make_async_remote_copy(
            src_ref=dst, dst_ref=dst, send_sem=send_sems.at[i], recv_sem=recv_sems.at[i],
            device_id=core, device_id_type=MESH).wait_recv()

    loads = [
        pltpu.make_async_copy(x_in, xg.at[0, rows_of(OWN)], load_sems.at[0]),
        pltpu.make_async_copy(g_in, xg.at[1, rows_of(OWN)], load_sems.at[1]),
        pltpu.make_async_copy(gw_in, gw, load_sems.at[2]),
        pltpu.make_async_copy(uw_in, uw, load_sems.at[3]),
        pltpu.make_async_copy(dw_in, dw, load_sems.at[4]),
    ]
    for load in loads:
        load.start()

    barrier = pltpu.get_barrier_semaphore()
    for device in everyone:
        pl.semaphore_signal(barrier, inc=1, device_id=device, device_id_type=MESH)
    pl.semaphore_wait(barrier, len(everyone))

    def tokens(block, plane=0):
        return xg.at[:, pl.ds(place(plane, block * BLOCK), BLOCK)]

    loads[0].wait()
    loads[1].wait()
    send("g_xl", tokens(OWN), tokens(PAR), to_xl)
    for way in "mp":
        send(f"gy_{way}_own", tokens(OWN), tokens(at_own[way]), same[way])

    def gather_par():
        arrived("g_xl", tokens(PAR))
        for way in "mp":
            send(f"gy_{way}_par", tokens(PAR), tokens(at_par[way]), same[way])

    def gather_far():
        send("gy_2_own", tokens(OWN), tokens(at_own["2"]), same["2"])
        send("gy_2_par", tokens(PAR), tokens(at_par["2"]), same["2"])

    def gather_depth():
        send("g_x2", tokens(OWN), tokens(OWN, 1), to_x2)
        send("g_xo", tokens(OWN), tokens(PAR, 1), to_xo)

    def gather_other():
        arrived("g_x2", tokens(OWN, 1))
        arrived("g_xo", tokens(PAR, 1))
        for way in "mp2":
            send(f"gy_{way}_oth0", tokens(OWN, 1), tokens(at_own[way], 1), same[way])
            send(f"gy_{way}_oth1", tokens(PAR, 1), tokens(at_par[way], 1), same[way])

    seen = set()
    source = {M0: "gy_p_own", Q0: "gy_m_own", M1: "gy_p_par", Q1: "gy_m_par", T0: "gy_2_own", T1: "gy_2_par"}

    def gathered(block):
        if block in source and block not in seen:
            seen.add(block)
            arrived(source[block], tokens(block))

    cols_own = pl.ds(multiple(k * HALF, 128), HALF)
    cols_par = pl.ds(multiple(kp * HALF, 128), HALF)

    def chunk(j):
        return pl.ds(BASE[j], CHUNKS[j])

    def products(j, cols, out):
        here = pl.ds(place(0, BASE[j]), CHUNKS[j])
        x, g = xg[0, here], xg[1, here]
        out[0, chunk(j)] = jnp.dot(x, gw[:, cols], preferred_element_type=F32).astype(BF16)
        out[1, chunk(j)] = jnp.dot(x, uw[:, cols], preferred_element_type=F32).astype(BF16)
        out[2, chunk(j)] = lax.dot_general(g, dw[cols, :], TRANS, preferred_element_type=F32).astype(BF16)

    def piece(j, zz):
        size = CHUNKS[j] // 4
        return pl.ds(multiple(BASE[j] + zz * size, 16), size)

    def act_piece(j, zz, plane=0):
        size = CHUNKS[j] // 4
        return pl.ds(multiple(place(plane, BASE[j]) + zz * size, 16), size)

    def slot(j):
        return pl.ds(BASE[j] // 4, CHUNKS[j] // 4)

    def whole(j):
        return core_recv.at[:, chunk(j)]

    def forward(j):
        for b in range(8):
            if b * BLOCK < BASE[j + 1] and (b + 1) * BLOCK > BASE[j]:
                gathered(b)
        if j == 0:
            for load in loads[2:]:
                load.wait()
        products(j, cols_par, core_send)
        send(f"core{j}", core_send.at[:, chunk(j)], whole(j), core)
        products(j, cols_own, part)

    def add_core(j):
        arrived(f"core{j}", whole(j))

        def add(zz):
            rows = piece(j, zz)
            part[:, rows] = (part[:, rows].astype(F32) + core_recv[:, rows].astype(F32)).astype(BF16)

        add(z2)
        send(f"relA{j}", part.at[pl.ds(0, 2), piece(j, z2)], relay.at[pl.ds(0, 2), slot(j)], to_a)
        send(f"relB{j}", part.at[pl.ds(2, 1), piece(j, z2)], relay.at[pl.ds(2, 1), slot(j)], to_b)
        add(za)
        add(zb)
        add(z)

    def add_relay(j):
        rows_a, rows_b = piece(j, za), piece(j, zb)
        arrived(f"relA{j}", relay.at[pl.ds(0, 2), slot(j)])
        part[0:2, rows_a] = (part[0:2, rows_a].astype(F32) + relay[0:2, slot(j)].astype(F32)).astype(BF16)
        send(f"finA{j}", part.at[:, rows_a], final.at[0, :, slot(j)], to_a)
        arrived(f"relB{j}", relay.at[pl.ds(2, 1), slot(j)])
        part[2:3, rows_b] = (part[2:3, rows_b].astype(F32) + relay[2:3, slot(j)].astype(F32)).astype(BF16)
        send(f"finB{j}", part.at[:, rows_b], final.at[1, :, slot(j)], to_b)

    def block(t, n, kk, j, zz, plane=0):
        return act.at[pl.ds(t, n), kk, act_piece(j, zz, plane)]

    def pass_on(name, ref, device):
        send(name, ref, ref, device)

    def activations(j):
        arrived(f"finA{j}", final.at[0, :, slot(j)])
        arrived(f"finB{j}", final.at[1, :, slot(j)])
        mine = piece(j, z)
        gate, up, grad = (
            part[t, mine].astype(F32) + final[0, t, slot(j)].astype(F32) + final[1, t, slot(j)].astype(F32)
            for t in range(3))
        sig = jax.nn.sigmoid(gate)
        here = act_piece(j, z)
        act[0, k, here] = (grad * up * sig * (1.0 + gate * (1.0 - sig))).astype(BF16)
        act[1, k, here] = (grad * gate * sig).astype(BF16)
        act[2, k, here] = (gate * sig * up).astype(BF16)
        pass_on(f"agA{j}", block(0, 3, k, j, z), to_a)
        pass_on(f"agB{j}", block(0, 3, k, j, z), to_b)
        send(f"agX{j}", block(0, 2, k, j, z), block(0, 2, k, j, z, 1), to_x2)
        pass_on(f"cOwn{j}", block(0, 3, k, j, z), core)

    def spread_own(j):
        arrived(f"agA{j}", block(0, 3, k, j, zb))
        pass_on(f"agA2{j}", block(0, 2, k, j, zb), to_a)
        pass_on(f"cB{j}", block(0, 3, k, j, zb), core)
        arrived(f"agB{j}", block(0, 3, k, j, za))
        pass_on(f"agB2{j}", block(2, 1, k, j, za), to_b)
        pass_on(f"cA{j}", block(0, 3, k, j, za), core)

    def spread_other(j):
        mine = block(0, 2, k, j, z, 1)
        arrived(f"agX{j}", mine)
        pass_on(f"ogA{j}", mine, to_a)
        pass_on(f"ogB{j}", mine, to_b)
        pass_on(f"oOwn{j}", mine, core)

    def hidden_rows(j, kk, plane):
        return act.at[2, kk, pl.ds(place(plane, BASE[j]), CHUNKS[j])]

    def end_own(j):
        arrived(f"agA2{j}", block(0, 2, k, j, z2))
        pass_on(f"cA2{j}", block(0, 2, k, j, z2), core)
        arrived(f"agB2{j}", block(2, 1, k, j, z2))
        pass_on(f"cB2{j}", block(2, 1, k, j, z2), core)
        send(f"agXh{j}", hidden_rows(j, k, 0), hidden_rows(j, k, 1), to_x2)

    def relay_other(j):
        arrived(f"ogA{j}", block(0, 2, k, j, zb, 1))
        pass_on(f"ogA2{j}", block(0, 1, k, j, zb, 1), to_a)
        pass_on(f"oB{j}", block(0, 2, k, j, zb, 1), core)
        arrived(f"ogB{j}", block(0, 2, k, j, za, 1))
        pass_on(f"ogB2{j}", block(1, 1, k, j, za, 1), to_b)
        pass_on(f"oA{j}", block(0, 2, k, j, za, 1), core)

    def end_other(j):
        arrived(f"ogA2{j}", block(0, 1, k, j, z2, 1))
        pass_on(f"oA2{j}", block(0, 1, k, j, z2, 1), core)
        arrived(f"ogB2{j}", block(1, 1, k, j, z2, 1))
        pass_on(f"oB2{j}", block(1, 1, k, j, z2, 1), core)

    def end_hidden(j):
        arrived(f"agXh{j}", hidden_rows(j, k, 1))
        pass_on(f"oH{j}", hidden_rows(j, k, 1), core)

    flushes = []

    def flush(src, dst):
        copy = pltpu.make_async_copy(src, dst, flush_sems.at[len(flushes)])
        copy.start()
        flushes.append(copy)

    def flush_act(j, plane):
        if BASE[j] < EARLY:
            return
        rows = pl.ds(place(plane, BASE[j]), CHUNKS[j])
        to_rows = pl.ds(place(plane, BASE[j]) - 2 * EARLY, CHUNKS[j])
        for t, out in enumerate((a0_out, a1_out, a2_out)):
            for kk in range(2):
                flush(act.at[t, kk, rows], out.at[to_rows, pl.ds(kk * HALF, HALF)])

    complete = set()

    def own_complete(j):
        if j in complete:
            return
        complete.add(j)
        arrived(f"cOwn{j}", block(0, 3, kp, j, z))
        arrived(f"cB{j}", block(0, 3, kp, j, za))
        arrived(f"cA{j}", block(0, 3, kp, j, zb))
        arrived(f"cA2{j}", block(0, 2, kp, j, z2))
        arrived(f"cB2{j}", block(2, 1, kp, j, z2))
        flush_act(j, 0)

    def other_complete(j):
        arrived(f"oOwn{j}", block(0, 2, kp, j, z, 1))
        arrived(f"oB{j}", block(0, 2, kp, j, za, 1))
        arrived(f"oA{j}", block(0, 2, kp, j, zb, 1))
        arrived(f"oA2{j}", block(0, 1, kp, j, z2, 1))
        arrived(f"oB2{j}", block(1, 1, kp, j, z2, 1))
        arrived(f"oH{j}", hidden_rows(j, kp, 1))
        flush_act(j, 1)

    gi_to = {PAR: to_xl, M0: same["m"], Q0: same["p"], M1: diag["m"], Q1: diag["p"], T0: same["2"], T1: diag["2"]}

    def input_grad(i):
        group = GI_GROUPS[i]
        first, end = group[0] * BLOCK, (group[-1] + 1) * BLOCK
        for j in range(len(CHUNKS)):
            if BASE[j] < end and BASE[j + 1] > first:
                own_complete(j)
        rows = pl.ds(first, end - first)
        act_rows = pl.ds(place(0, first), end - first)
        total = None
        for t, w in enumerate((gw, uw)):
            for kk in range(2):
                term = lax.dot_general(act[t, kk, act_rows], w[:, kk * HALF:(kk + 1) * HALF], TRANS,
                                       preferred_element_type=F32)
                total = term if total is None else total + term
        gi_send[rows] = total.astype(BF16)
        for b in group:
            if b != OWN:
                send(f"gi{b}", gi_send.at[rows_of(b)], gi_recv.at[b], gi_to[b])

    def flush_tokens():
        for way in "mp2":
            arrived(f"gy_{way}_oth0", tokens(at_own[way], 1))
            arrived(f"gy_{way}_oth1", tokens(at_par[way], 1))
        late = pl.ds(2 * EARLY, 2 * (PLANE - EARLY))
        flush(xg.at[0, late], x_out)
        flush(xg.at[1, late], g_out)

    wg_copies = []

    def wg_slot():
        n = len(wg_copies)
        if n >= 4:
            wg_copies[n - 4].wait()
        return n % 4

    def wg_store(src, dst):
        copy = pltpu.make_async_copy(src, dst, wg_sems.at[len(wg_copies)])
        copy.start()
        wg_copies.append(copy)

    early = pl.ds(0, 2 * EARLY)

    def weight_grad_in(t, m):
        i = wg_slot()
        lhs = xg[0, early, m * 256:(m + 1) * 256]
        for kk in range(2):
            wg[i, :, kk * HALF:(kk + 1) * HALF] = lax.dot_general(
                lhs, act[t, kk, early], OVER_TOKENS, preferred_element_type=F32).astype(BF16)
        wg_store(wg.at[i], (p0_out, p1_out)[t].at[pl.ds(m * 256, 256)])

    def weight_grad_down(kk, m):
        i = wg_slot()
        size = min(256, HALF - m * 256)
        wg[i, :size, :WIDTH] = lax.dot_general(
            act[2, kk, early, m * 256:m * 256 + size], xg[1, early], OVER_TOKENS,
            preferred_element_type=F32).astype(BF16)
        wg_store(wg.at[i, pl.ds(0, size), pl.ds(0, WIDTH)], p2_out.at[pl.ds(kk * HALF + m * 256, size)])

    stages = {
        "G2": gather_par, "G3": gather_far, "G4": gather_depth, "G5": gather_other, "GF": flush_tokens,
        "F": forward, "P": add_core, "R": add_relay, "C": activations, "D1": spread_own, "D2": spread_other,
        "D3": end_own, "D4": relay_other, "D5": end_other, "D6": end_hidden, "H": other_complete,
        "E": input_grad, "W": weight_grad_in, "V": weight_grad_down,
    }
    for name, *index in ORDER:
        stages[name](*index)

    total = gi_send[rows_of(OWN)].astype(F32)
    for b in range(1, 8):
        arrived(f"gi{b}", gi_recv.at[b])
        total = total + gi_recv[b].astype(F32)
    gin_out[...] = total.astype(BF16)
    for copy in started:
        copy.wait_send()
    for copy in flushes + wg_copies[-4:]:
        copy.wait()


def per_device(inputs, grad_out, gate_weight, up_weight, down_weight):
    hbm = pl.BlockSpec(memory_space=pl.ANY)
    n = len(NAMES)
    tokens = 2 * PLANE
    late = tokens - 2 * EARLY
    grad_in, x, g, gate_act, up_act, hidden, gate_early, up_early, down_early = pl.pallas_call(
        kernel,
        out_shape=(
            jax.ShapeDtypeStruct((BLOCK, WIDTH), BF16),
            jax.ShapeDtypeStruct((late, WIDTH), BF16),
            jax.ShapeDtypeStruct((late, WIDTH), BF16),
            jax.ShapeDtypeStruct((late, HID), BF16),
            jax.ShapeDtypeStruct((late, HID), BF16),
            jax.ShapeDtypeStruct((late, HID), BF16),
            jax.ShapeDtypeStruct((WIDTH, HID), BF16),
            jax.ShapeDtypeStruct((WIDTH, HID), BF16),
            jax.ShapeDtypeStruct((HID, WIDTH), BF16),
        ),
        in_specs=[hbm] * 5,
        out_specs=(pl.BlockSpec(memory_space=pltpu.VMEM),) + (hbm,) * 8,
        scratch_shapes=[
            pltpu.VMEM((WIDTH, HID), BF16),
            pltpu.VMEM((WIDTH, HID), BF16),
            pltpu.VMEM((HID, WIDTH), BF16),
            pltpu.VMEM((2, tokens, WIDTH), BF16),
            pltpu.VMEM((3, 2, tokens, HALF), BF16),
            pltpu.VMEM((3, PLANE, HALF), BF16),
            pltpu.VMEM((3, PLANE, HALF), BF16),
            pltpu.VMEM((3, PLANE, HALF), BF16),
            pltpu.VMEM((3, PLANE // 4, HALF), BF16),
            pltpu.VMEM((2, 3, PLANE // 4, HALF), BF16),
            pltpu.VMEM((PLANE, WIDTH), BF16),
            pltpu.VMEM((8, BLOCK, WIDTH), BF16),
            pltpu.VMEM((4, 256, HID), BF16),
            pltpu.SemaphoreType.DMA((n,)),
            pltpu.SemaphoreType.DMA((n,)),
            pltpu.SemaphoreType.DMA((5,)),
            pltpu.SemaphoreType.DMA((N_FLUSH,)),
            pltpu.SemaphoreType.DMA((16,)),
        ],
        compiler_params=pltpu.CompilerParams(
            collective_id=0, has_side_effects=True, vmem_limit_bytes=62 * 2**20),
        name="ffn_exchange",
    )(inputs, grad_out, gate_weight, up_weight, down_weight)

    def weight_grad(a, b, rest):
        late_sum = lax.dot_general(a, b, OVER_TOKENS, preferred_element_type=F32)
        return (late_sum + rest.astype(F32)).astype(BF16)

    return (
        grad_in,
        weight_grad(x, gate_act, gate_early),
        weight_grad(x, up_act, up_early),
        weight_grad(hidden, g, down_early),
    )


def solution(mesh):
    in_specs = (
        P(("depth", "col"), "row"),
        P(("depth", "col"), "row"),
        P("row", "col"),
        P("row", "col"),
        P("col", "row"),
    )
    out_specs = (P(("depth", "col"), "row"), P("row", "col"), P("row", "col"), P("col", "row"))
    return jax.shard_map(
        per_device, mesh=mesh, in_specs=in_specs, out_specs=out_specs, check_vma=False
    )
```

time: 486 us -> 155 us (0.32)
  waiting for transfers between devices: 396 us -> 0 us
  Pallas kernels: 0 us -> 135 us
  matrix products: 49.4 us -> 17.7 us
  local copies, waits for them, and re-layouts: 17.6 us -> 0.71 us
  between operations: 14.2 us -> 0.71 us
    all_gather x5 -> x0, waiting for transfers between devices: 221 us -> none  [the longest x1 56.5 us: per_device(): lax.all_gather(up_half.astype(jnp.bfloat16), 'depth', axis=1, tiled=True)]
    pallas_call x0 -> x1, Pallas kernels: none -> 135 us  [per_device(): pl.pallas_call(kernel, out_shape=(jax.ShapeDtypeStruct((BLOCK, WIDTH), BF...]
    psum x1 -> x0, waiting for transfers between devices: 103 us -> none  [per_device(): lax.psum(up_part.astype(jnp.bfloat16), 'row').astype(jnp.float32)]
    reduce_scatter x1 -> x0, waiting for transfers between devices: 71.1 us -> none  [per_device(): lax.psum_scatter((lax.dot_general(grad_gate_act, gate_cols, contract_last...]
    dot_general x8 -> x3, matrix products: 49.4 us -> 17.7 us  [weight_grad(): late_sum = lax.dot_general(a, b, OVER_TOKENS, preferred_element_type=F32)]
    unnamed x17 -> x15, local copies, waits for them, and re-layouts: 17.6 us -> 0.71 us
  transfers between devices with their start and end apart: 7 -> 0, of which waited for: 7 -> 0; matrix products, arithmetic and copies ran while one was open for 10% -> 0% of each run, Pallas kernels for 0% -> 0%
where the time goes in v2:
time: 155 us; the launch traced here: 154 us
  Pallas kernels  135 us (87%)
  matrix products  17.7 us (11%)
    pallas_call x1, Pallas kernels, per_device(): pl.pallas_call(kernel, out_shape=(jax.ShapeDtypeStruct((BLOCK, WIDTH), BF...  135 us
    dot_general x3, matrix products, weight_grad(): late_sum = lax.dot_general(a, b, OVER_TOKENS, preferred_element_type=F32)  17.7 us

profile of v2, /device:TPU:73, one launch (start us, length us, event | category | flops | bytes accessed | tf_op | source)
XLA Modules:
  0.0 153.6 jit_solution(10366819620597585711)
XLA Ops:
  0.6 134.5 %ffn_exchange.1 = (bf16[96,1024]{1,0:T(8,128)(2,1)}, bf16[768,1024]{1,0:T(8,128)(2,1)}, bf16[768,1024]{1,0:T(8,128)(2,1)}, bf16[768,1792]{1,0:T(8,128)(2,1)}, bf...) custom-call(bf16[96,1024]{1,0:T(8,128)(2,1)} %x_in.1, ...), custom_call_target="tpu_custom_call" | custom-call | tf_op jit(solution)/shard_map/ffn_exchange/pallas_call | solution.py:404
  135.2 0.0 copy-start.2
  135.2 0.0 copy-start.4
  135.2 0.0 copy-start.6
  135.2 8.4 %add_convert_fusion.2 = bf16[1024,1792]{1,0:T(8,128)(2,1)} fusion(bf16[1024,1792]{1,0:T(8,128)(2,1)} %get-tuple-element.16, bf16[768,1024]{1,0:T(8,128)(2,1)} %get-tuple-element.14, bf16[768,1792]{1,0:T(8,128)(2,1)} %get-tuple-element.15), kind=kOutput, calls=%fused_computation.2 | convolution fusion | flops 2824077312 | bytes 11665408 | tf_op jit(solution)/shard_map/dot_general | solution.py:445
  143.6 0.0 copy-done.2
  143.6 0.0 copy-done.4
  143.6 0.0 copy-done.6
  143.6 0.0 copy-start.1
  143.6 0.0 copy-start.3
  143.6 0.0 copy-start.5
  143.6 4.7 %add_convert_fusion.1 = bf16[1024,1792]{1,0:T(8,128)(2,1)} fusion(bf16[1024,1792]{1,0:T(8,128)(2,1)S(1)} %copy-done.2, bf16[768,1024]{1,0:T(8,128)(2,1)S(1)} %copy-done.6, bf16[768,1792]{1,0:T(8,128)(2,1)S(1)} %copy-done.4), kind=kOutput, calls=%fused_computation.1 | convolution fusion | flops 2824077312 | bytes 11665408 | tf_op jit(solution)/shard_map/dot_general | solution.py:445
  148.3 0.0 copy-done.1
  148.3 0.0 copy-done.3
  148.3 0.0 copy-done.5
  148.3 0.0 copy-start
  148.3 4.6 %add_convert_fusion = bf16[1792,1024]{1,0:T(8,128)(2,1)} fusion(bf16[1792,1024]{1,0:T(8,128)(2,1)S(1)} %copy-done.1, bf16[768,1792]{1,0:T(8,128)(2,1)S(1)} %copy-done.3, bf16[768,1024]{1,0:T(8,128)(2,1)S(1)} %copy-done.5), kind=kOutput, calls=%fused_computation | convolution fusion | flops 2824077312 | bytes 11665408 | tf_op jit(solution)/shard_map/dot_general | solution.py:445
  152.9 0.0 copy-done
  152.9 0.7 copy.10
Async XLA Ops:
  135.2 8.4 %copy-start.2 = (bf16[1024,1792]{1,0:T(8,128)(2,1)S(1)}, bf16[1024,1792]{1,0:T(8,128)(2,1)}, u32[]{:S(2)}) copy-start(bf16[1024,1792]{1,0:T(8,128)(2,1)} %get-tuple-element.18) | copy-start | bytes 11010052
  135.2 8.4 %copy-start.4 = (bf16[768,1792]{1,0:T(8,128)(2,1)S(1)}, bf16[768,1792]{1,0:T(8,128)(2,1)}, u32[]{:S(2)}) copy-start(bf16[768,1792]{1,0:T(8,128)(2,1)} %get-tuple-element.17) | copy-start | bytes 8257540
  135.2 8.4 %copy-start.6 = (bf16[768,1024]{1,0:T(8,128)(2,1)S(1)}, bf16[768,1024]{1,0:T(8,128)(2,1)}, u32[]{:S(2)}) copy-start(bf16[768,1024]{1,0:T(8,128)(2,1)} %get-tuple-element.14) | copy-start | bytes 4718596
  143.6 4.7 %copy-start.1 = (bf16[1792,1024]{1,0:T(8,128)(2,1)S(1)}, bf16[1792,1024]{1,0:T(8,128)(2,1)}, u32[]{:S(2)}) copy-start(bf16[1792,1024]{1,0:T(8,128)(2,1)} %get-tuple-element.21) | copy-start | bytes 11010052
  143.6 4.7 %copy-start.3 = (bf16[768,1792]{1,0:T(8,128)(2,1)S(1)}, bf16[768,1792]{1,0:T(8,128)(2,1)}, u32[]{:S(2)}) copy-start(bf16[768,1792]{1,0:T(8,128)(2,1)} %get-tuple-element.19) | copy-start | bytes 8257540
  143.6 4.7 %copy-start.5 = (bf16[768,1024]{1,0:T(8,128)(2,1)S(1)}, bf16[768,1024]{1,0:T(8,128)(2,1)}, u32[]{:S(2)}) copy-start(bf16[768,1024]{1,0:T(8,128)(2,1)} %get-tuple-element.20) | copy-start | bytes 4718596
  148.3 4.6 %copy-start = (bf16[96,1024]{1,0:T(8,128)(2,1)S(1)}, bf16[96,1024]{1,0:T(8,128)(2,1)}, u32[]{:S(2)}) copy-start(bf16[96,1024]{1,0:T(8,128)(2,1)} %get-tuple-element.26) | copy-start | bytes 589828
